TPU v7x, 128 devices: a whole 4x4x4 slice. The times are simulated.
128 devices in a mesh: rep: 16 (over z_lo, y, core), tp: 8 (over z_hi, x).
Axes of the slice: x: 4, y: 4, z: 4 (z_hi: 2, z_lo: 2; z = z_hi * 2 + z_lo), core: 2. Of those that a mesh axis runs over, the one named last changes fastest.
Arguments:
- normed: bfloat16 [64, 128, 4096], P('rep', None, 'tp'), may hold values from -6 to 6
- documents: int32 [64, 128], P('rep'), may hold values from 0 to 15, never falling along the last dimension, each value on 1 to 64 neighbouring positions
- cotangent: bfloat16 [64, 128, 4096], P('rep'), may hold values from -6 to 6
- w_query: bfloat16 [16, 4096, 4096], P('rep', None, 'tp'), may hold values from -6 to 6
- w_key: bfloat16 [16, 4096, 1024], P('rep', None, 'tp'), may hold values from -6 to 6
- w_value: bfloat16 [16, 4096, 1024], P('rep', None, 'tp'), may hold values from -6 to 6
- w_out: bfloat16 [16, 4096, 4096], P('rep', 'tp'), may hold values from -6 to 6
- step_index: int32 [1], replicated, may hold values from 0 to 63
Outputs:
- layer_out: bfloat16 [64, 128, 4096], P('rep', None, 'tp')
- new_query: bfloat16 [16, 4096, 4096], P('rep', None, 'tp')
- new_key: bfloat16 [16, 4096, 1024], P('rep', None, 'tp')
- new_value: bfloat16 [16, 4096, 1024], P('rep', None, 'tp')
- new_out: bfloat16 [16, 4096, 4096], P('rep', 'tp')
All inputs are finite; a program needn't handle non-finite values.
Results may differ from a plain program's by a relative error of at most 0.017.
Values may be sent and summed in bfloat16 or wider, within the bound.
A program may use at most 192 MiB of HBM per device.

v0:
```python
import math

import jax
import jax.numpy as jnp
from jax import lax
from jax.sharding import PartitionSpec as P

HEAD = 128


def for_sending(array):
    return jax.tree.map(lambda a: a.astype(jnp.bfloat16) if a.dtype == jnp.float32 else a, array)


def passed_along(value, axis, steps):
    count = lax.axis_size(axis)
    pairs = [(source, (source + steps) % count) for source in range(count)]
    return lax.ppermute(value, axis, pairs)


def rotate(values, positions):
    half_dim = values.shape[-1] // 2
    frequency = 500000.0 ** (-jnp.arange(half_dim, dtype=jnp.float32) / half_dim)
    angles = positions[:, None].astype(jnp.float32) * frequency[None, :]
    cosine = jnp.cos(angles)[None, :, None, :]
    sine_part = jnp.sin(angles)[None, :, None, :]
    front_part = values[..., :half_dim]
    second = values[..., half_dim:]
    return jnp.concatenate(
        [front_part * cosine - second * sine_part, second * cosine + front_part * sine_part],
        axis=-1,
    )


def attend(params, normed, documents, head_dim):
    w_query, w_key, w_value, w_out = params
    batch, length, width = normed.shape
    flat = normed.reshape(batch * length, width)
    scale_in = 1.0 / math.sqrt(width)
    q_heads = w_query.shape[1] // head_dim
    kv_heads = w_key.shape[1] // head_dim
    positions = jnp.arange(length)
    queries = jnp.dot(flat, w_query, preferred_element_type=jnp.float32) * scale_in
    queries = rotate(queries.reshape(batch, length, q_heads, head_dim), positions).astype(
        jnp.bfloat16
    )
    keys_all = jnp.dot(flat, w_key, preferred_element_type=jnp.float32) * scale_in
    keys_all = rotate(keys_all.reshape(batch, length, kv_heads, head_dim), positions).astype(
        jnp.bfloat16
    )
    values_all = (jnp.dot(flat, w_value, preferred_element_type=jnp.float32) * scale_in).astype(
        jnp.bfloat16
    )
    values_all = values_all.reshape(batch, length, kv_heads, head_dim)
    group_size = q_heads // kv_heads
    queries = queries.reshape(batch, length, kv_heads, group_size, head_dim)
    scores = jnp.einsum(
        "bqkgd,bskd->bkgqs", queries, keys_all, preferred_element_type=jnp.float32
    ) / math.sqrt(head_dim)
    causal = positions[None, :] <= positions[:, None]
    same_doc = documents[:, :, None] == documents[:, None, :]
    allowed = jnp.logical_and(causal[None], same_doc)
    scores = jnp.where(allowed[:, None, None], scores, -1000000000.0)
    probs = jax.nn.softmax(scores, axis=-1).astype(jnp.bfloat16)
    mixed = jnp.einsum(
        "bkgqs,bskd->bqkgd", probs, values_all, preferred_element_type=jnp.float32
    ).astype(jnp.bfloat16)
    mixed = mixed.reshape(batch * length, q_heads * head_dim)
    output = jnp.dot(mixed, w_out, preferred_element_type=jnp.float32) * scale_in
    return output.reshape(batch, length, width)


def pack_all(members):
    return jnp.concatenate([member.reshape(-1) for member in members]).reshape(-1, 128)


def unpack_all(packed, layouts):
    linear = packed.reshape(-1)
    pieces = []
    offset = 0
    for layout in layouts:
        amount = layout[0] * layout[1]
        pieces.append(linear[offset : offset + amount].reshape(layout))
        offset = offset + amount
    return pieces


def apply_step(weights, gradients, rate_now):
    return (weights.astype(jnp.float32) - rate_now * gradients.astype(jnp.float32)).astype(
        jnp.bfloat16
    )


def shift_params(data, level, levels):

    def make_branch(distance):
        return lambda payload: jax.tree.map(
            lambda part, own: part.astype(own.dtype),
            passed_along(for_sending(payload), "rep", distance),
            payload,
        )

    return lax.switch(level, [make_branch(2**exponent) for exponent in range(levels)], data)


def shift_grads(data, level, levels):

    def make_branch(distance):
        return lambda payload: jax.tree.map(
            lambda part, own: part.astype(own.dtype),
            passed_along(for_sending(payload), "rep", distance),
            payload,
        )

    return lax.switch(level, [make_branch(2**exponent) for exponent in range(levels)], data)


def per_device(normed, documents, cotangent, w_query, w_key, w_value, w_out, step_index):
    levels = lax.axis_size("rep").bit_length() - 1
    level = step_index[0] % levels
    rate_now = 3.0 * 32.0 / (32.0 + step_index[0].astype(jnp.float32))
    params = (w_query[0], w_key[0], w_value[0], w_out[0])
    layouts = [member.shape for member in params]
    packed_w = pack_all(params)
    peer_w = shift_params(packed_w, level, levels)
    whole = lax.all_gather(normed, "tp", axis=2, tiled=True)

    def local(weights):
        return attend(weights, whole, documents, HEAD)

    result, pull = jax.vjp(local, params)
    grads = pull(cotangent.astype(jnp.float32))[0]
    grads = tuple((grad for grad in grads))
    layer_out = lax.psum_scatter(result, "tp", scatter_dimension=2, tiled=True).astype(jnp.bfloat16)
    packed_g = pack_all(grads)
    own_updated = apply_step(packed_w, packed_g, rate_now)
    peer_g = shift_grads(packed_g, level, levels)
    peer_updated = apply_step(peer_w, peer_g, rate_now)
    averaged = (0.5 * (own_updated.astype(jnp.float32) + peer_updated.astype(jnp.float32))).astype(
        jnp.bfloat16
    )
    new_query, new_key, new_value, new_out = unpack_all(averaged, layouts)
    return (layer_out, new_query[None], new_key[None], new_value[None], new_out[None])


def solution(mesh):
    in_specs = (
        P("rep", None, "tp"),
        P("rep", None),
        P("rep", None, None),
        P("rep", None, "tp"),
        P("rep", None, "tp"),
        P("rep", None, "tp"),
        P("rep", "tp", None),
        P(),
    )
    out_specs = (
        P("rep", None, "tp"),
        P("rep", None, "tp"),
        P("rep", None, "tp"),
        P("rep", None, "tp"),
        P("rep", "tp", None),
    )
    return jax.shard_map(
        per_device, mesh=mesh, in_specs=in_specs, out_specs=out_specs, check_vma=False
    )
```

profile of v0, /device:TPU:1, one launch (start us, length us, event | category | flops | bytes accessed | tf_op | source)
XLA Modules:
  0.0 719.9 jit_solution(6846959260733572285)
XLA Ops:
  13.6 4.6 fusion.13
  19.4 5.6 copy.54
  25.0 4.2 copy.53
  29.3 36.3 %maximum_bitcast_fusion = bf16[40960,128]{1,0:T(8,128)(2,1)S(1)} fusion(bf16[2097152]{0:T(1024)(128)(2,1)} %bitcast.188, bf16[524288]{0:T(1024)(128)(2,1)S(1)} %bitcast.210, bf16[524288]{0:T(1024)(128)(2,1)S(1)} %bitcast.205, bf16[2097152]{0:T(1024)(128)(2,1)} %bitcast.190), kind=kLoop, calls=%fused_computation.3 | loop fusion | flops 41943040 | bytes 20971520 | tf_op jit(solution)/shard_map/reshape | solution.py:74
  65.6 230.5 %conditional.8 = (bf16[40960,128]{1,0:T(8,128)(2,1)}) conditional(s32[]{:T(128)} %clamp.4, bf16[40960,128]{1,0:T(8,128)(2,1)S(1)} %maximum_bitcast_fusion, bf16[40960,128]{1,0:T(8,128)(2,1)S(1)} %maximum_bitcast_fusion, bf16[40960,128]{1,0:T(8,128)(2,1)S(1)} %maximum_bitcast_fusion, ...), branch_computations={%region_4.5_spmd, %region_5.6_spmd, %region_6.7_spmd, %region_7.8_... | conditional | bytes 41943088
  67.9 228.0 %collective-permute-done.1 = bf16[40960,128]{1,0:T(8,128)(2,1)} collective-permute-done((bf16[40960,128]{1,0:T(8,128)(2,1)S(1)}, bf16[40960,128]{1,0:T(8,128)(2,1)}, u32[]{:S(2)}, u32[]{:S(2)}) %collective-permute-start.1) | collective-permute-done | bytes 10485792 | tf_op jit(solution)/shard_map/cond/branch_1_fun/ppermute | solution.py:18
  297.3 4.2 fusion.23
  301.5 3.4 convolution_multiply_fusion.2
  314.8 4.6 fusion.8
  319.4 8.4 %convolution_multiply_fusion = f32[512,4096]{1,0:T(8,128)} fusion(bf16[1,512,4096]{2,1,0:T(8,128)(2,1)} %param.22, bf16[64,8,4,128]{3,2,1,0:T(4,128)(2,1)S(1)} %bitcast.208), kind=kOutput, calls=%fused_computation.6 | convolution fusion | flops 2149580800 | bytes 13107200 | tf_op jit(solution)/shard_map/jvp()/dot_general | solution.py:69
  327.8 3.3 copy.57
  332.8 4.0 fusion.2
  341.2 6.6 fusion
  347.7 6.5 copy.31
  354.2 6.4 copy.56
  360.6 36.3 %maximum_bitcast_fusion.1 = bf16[40960,128]{1,0:T(8,128)(2,1)S(1)} fusion(bf16[2097152]{0:T(1024)(128)(2,1)} %bitcast.192, bf16[524288]{0:T(1024)(128)(2,1)S(1)} %bitcast.203, bf16[524288]{0:T(1024)(128)(2,1)S(1)} %bitcast.201, bf16[2097152]{0:T(1024)(128)(2,1)} %bitcast.194), kind=kLoop, calls=%fused_computation.4 | loop fusion | flops 41943040 | bytes 20971520 | tf_op jit(solution)/shard_map/reshape | solution.py:74
  396.9 213.2 %conditional.9 = (bf16[40960,128]{1,0:T(8,128)(2,1)}) conditional(s32[]{:T(128)} %clamp.4, bf16[40960,128]{1,0:T(8,128)(2,1)S(1)} %maximum_bitcast_fusion.1, bf16[40960,128]{1,0:T(8,128)(2,1)S(1)} %maximum_bitcast_fusion.1, bf16[40960,128]{1,0:T(8,128)(2,1)S(1)} %maximum_bitcast_fusion.1, ...), branch_computations={%region_8.9_spmd, %region_9.10_spmd, %region_10.11_spmd, %region_1... | conditional | bytes 41943088
  397.0 213.1 %collective-permute-done.5 = bf16[40960,128]{1,0:T(8,128)(2,1)} collective-permute-done((bf16[40960,128]{1,0:T(8,128)(2,1)S(1)}, bf16[40960,128]{1,0:T(8,128)(2,1)}, u32[]{:S(2)}, u32[]{:S(2)}) %collective-permute-start.5) | collective-permute-done | bytes 10485792 | tf_op jit(solution)/shard_map/cond/branch_1_fun/ppermute | solution.py:18
  610.1 40.0 %multiply_convert_fusion = bf16[40960,128]{1,0:T(8,128)(2,1)} fusion(bf16[40960,128]{1,0:T(8,128)(2,1)} %get-tuple-element.56, bf16[40960,128]{1,0:T(8,128)(2,1)} %get-tuple-element.55, f32[]{:T(128)S(6)} %div.78, bf16[2097152]{0:T(1024)(128)(2,1)} %bitcast.193, bf16[524288]{0:T(1024)(128)(2,1)S(1)} %bitcast.204, bf16[524288]{0:T(1024)(128)(2,1)S(1)} %bitcast.202, ...), kind=kLoop, calls=%fused_computation | loop fusion | flops 162529280 | bytes 52428804 | tf_op jit(solution)/shard_map/convert_element_type | solution.py:139
  650.1 5.9 fusion.59
  656.0 7.3 %broadcast_in_dim_reshape.15 = bf16[1,512,4096]{2,1,0:T(8,128)(2,1)} reshape(bf16[16384,128]{1,0:T(8,128)(2,1)} %get-tuple-element.35) | data formatting | bytes 8388608 | tf_op jit(solution)/shard_map/broadcast_in_dim;reshape | solution.py:143
  663.3 7.5 %broadcast_in_dim_reshape.12 = bf16[1,4096,512]{2,1,0:T(8,128)(2,1)} reshape(bf16[16384,128]{1,0:T(8,128)(2,1)} %get-tuple-element.36) | data formatting | bytes 8388608 | tf_op jit(solution)/shard_map/broadcast_in_dim;reshape | solution.py:143
  670.8 3.0 slice_bitcast_fusion
  673.8 37.0 %reduce-scatter.2.cloned.1.call-done = f32[4,128,512]{2,1,0:T(8,128)} async-done(((f32[4,128,4096]{2,1,0:T(8,128)}), f32[4,128,512]{2,1,0:T(8,128)}) %reduce-scatter.2.cloned.1.call-update) | async-done | bytes 1048592 | tf_op jit(solution)/shard_map/reduce_scatter | solution.py:134
  (61 shorter events, 28.2 us)
Async XLA Ops:
  7.2 290.1 %all-gather.2.cloned.1.call-start = ((), (), s32[]{:S(2)}) async-start(), calls=%async_computation.1 | async-start | bytes 4718592 | tf_op jit(solution)/shard_map/all_gather | solution.py:126
  7.9 702.9 %reduce-scatter.2.cloned.1.call-start = ((), (), s32[]{:S(2)}) async-start(), calls=%async_computation.2 | async-start | bytes 9437184 | tf_op jit(solution)/shard_map/reduce_scatter | solution.py:134
  11.6 2.0 copy-start.2
  18.2 11.1 %copy-start.3 = (bf16[1,4096,128]{2,1,0:T(8,128)(2,1)S(1)}, bf16[1,4096,128]{2,1,0:T(8,128)(2,1)}, u32[]{:S(2)}) copy-start(bf16[1,4096,128]{2,1,0:T(8,128)(2,1)} %param.20) | copy-start | bytes 3145732
  18.2 11.1 %copy-start.4 = (bf16[1,4096,128]{2,1,0:T(8,128)(2,1)S(1)}, bf16[1,4096,128]{2,1,0:T(8,128)(2,1)}, u32[]{:S(2)}) copy-start(bf16[1,4096,128]{2,1,0:T(8,128)(2,1)} %param.21) | copy-start | bytes 3145732
  19.4 5.6 copy-start.5
  29.3 266.8 %copy-start.10 = (s32[4,128]{1,0:T(4,128)S(1)}, s32[4,128]{1,0:T(4,128)}, u32[]{:S(2)}) copy-start(s32[4,128]{1,0:T(4,128)} %param.17) | copy-start | bytes 6148
  65.6 230.2 %collective-permute-start.1 = (bf16[40960,128]{1,0:T(8,128)(2,1)S(1)}, bf16[40960,128]{1,0:T(8,128)(2,1)}, u32[]{:S(2)}, u32[]{:S(2)}) collective-permute-start(bf16[40960,128]{1,0:T(8,128)(2,1)S(1)} %param.1), channel_id=1, source_target_pairs={{0,16},{8,24},{16,32},{24,40},{32,48},{40,56},{48,64},{56,72},{64,... | collective-permute-start | bytes 31457288 | tf_op jit(solution)/shard_map/cond/branch_1_fun/ppermute | solution.py:18
  297.3 7.7 %copy-start = (bf16[4,128,4096]{2,1,0:T(8,128)(2,1)S(1)}, bf16[4,128,4096]{2,1,0:T(8,128)(2,1)}, u32[]{:S(2)}) copy-start(bf16[4,128,4096]{2,1,0:T(8,128)(2,1)} %all-gather.2.cloned.1.call-done) | copy-start | bytes 12582916
  297.3 7.7 %copy-start.6 = (bf16[1,4096,512]{2,1,0:T(8,128)(2,1)S(1)}, bf16[1,4096,512]{2,1,0:T(8,128)(2,1)}, u32[]{:S(2)}) copy-start(bf16[1,4096,512]{2,1,0:T(8,128)(2,1)} %param.19) | copy-start | bytes 12582916
  307.7 2.7 copy-start.9
  307.7 3.0 copy-start.7
  308.3 3.8 copy-start.8
  319.4 12.0 %copy-start.1 = (bf16[4,128,4096]{2,1,0:T(8,128)(2,1)S(1)}, bf16[4,128,4096]{2,1,0:T(8,128)(2,1)}, u32[]{:S(2)}) copy-start(bf16[4,128,4096]{2,1,0:T(8,128)(2,1)} %all-gather.2.cloned.1.call-done) | copy-start | bytes 12582916
  396.9 213.2 %collective-permute-start.5 = (bf16[40960,128]{1,0:T(8,128)(2,1)S(1)}, bf16[40960,128]{1,0:T(8,128)(2,1)}, u32[]{:S(2)}, u32[]{:S(2)}) collective-permute-start(bf16[40960,128]{1,0:T(8,128)(2,1)S(1)} %param.5), channel_id=1, source_target_pairs={{0,16},{8,24},{16,32},{24,40},{32,48},{40,56},{48,64},{56,72},{64,... | collective-permute-start | bytes 31457288 | tf_op jit(solution)/shard_map/cond/branch_1_fun/ppermute | solution.py:18
Sparse Core Ops, SparseCore 0:
  10.2 76.6 all-gather.1
  360.7 350.0 reduce-scatter.1
where the time goes:
time: 726 us; the launch traced here: 720 us
  waiting for transfers between devices  479 us (66%)
  other arithmetic  122 us (17%)
  local copies, waits for them, and re-layouts  56.8 us (8%)
  matrix products  44.3 us (6%)
  between operations  15.4 us (2%)
    ppermute x2, waiting for transfers between devices, passed_along(): return lax.ppermute(value, axis, pairs)  441 us
    reshape x2, other arithmetic, pack_all(): jnp.concatenate([member.reshape(-1) for member in members]).reshape(-1, 128)  72.6 us
    convert_element_type x1, other arithmetic, per_device(): (0.5 * (own_updated.astype(jnp.float32) + peer_updated.astype(jnp.float32...  40 us
    reduce_scatter x1, waiting for transfers between devices, per_device(): lax.psum_scatter(result, 'tp', scatter_dimension=2, tiled=True)  37 us
    unnamed x26, local copies, waits for them, and re-layouts  21.5 us
    dot_general x3, matrix products, attend(): jnp.dot(mixed, w_out, preferred_element_type=jnp.float32) * scale_in  17.5 us
  transfers between devices with their start and end apart: 4, of which 3 were waited for; matrix products, arithmetic and copies ran while one was open for 22% of the time, Pallas kernels for 0%

commit v1 on v0

v1 whole, which is shorter than its diff:
```python
import functools
import math

import jax
import jax.numpy as jnp
import numpy as np
from jax import lax
from jax.experimental import pallas as pl
from jax.experimental.pallas import tpu as pltpu
from jax.sharding import PartitionSpec as P

HEAD = 128
SEQS = 4
SEQ = 128
TOKENS = SEQS * SEQ
X_CHIPS = 4
Y_CHIPS = 4
TP = 8
D = 4096
SLAB = D // TP
Q_HEADS = 4
Q_COLS = Q_HEADS * HEAD
QKV = Q_COLS + 2 * HEAD
SCALE = 1.0 / math.sqrt(D)
SCORE_SCALE = 1.0 / math.sqrt(HEAD)
MESH = pl.DeviceIdType.MESH
F32 = jnp.float32
BF16 = jnp.bfloat16


def rotation_tables():
    half = HEAD // 2
    frequency = (500000.0 ** (-np.arange(half, dtype=np.float64) / half)).astype(np.float32)
    angles = np.arange(SEQ, dtype=np.float32)[:, None] * frequency[None, :]
    cosine, sine = np.cos(angles), np.sin(angles)
    return (
        np.concatenate([cosine, cosine], axis=1).astype(np.float32),
        np.concatenate([-sine, sine], axis=1).astype(np.float32),
    )


def dot(a, b, contract):
    return lax.dot_general(
        a, b, (((contract[0],), (contract[1],)), ((), ())), preferred_element_type=F32
    )


def turned(values, cosine, sine):
    return values * cosine + pltpu.roll(values, HEAD // 2, 1) * sine


def front_kernel(
    x_in, cot_in, wq_in, wk_in, wv_in, wo_in, docs, cos_ref, sin_ref,
    x_out, mixed_out, dqkv_out,
    x_all, cot, w_qkv, w_o, acc, d_mixed,
    send_sems, recv_sems, load_sems, store_sems,
):
    me = lax.axis_index("tp")
    x, z = me % X_CHIPS, me // X_CHIPS
    right = z * X_CHIPS + (x + 1) % X_CHIPS
    left = z * X_CHIPS + (x + 3) % X_CHIPS
    far = z * X_CHIPS + (x + 2) % X_CHIPS
    across = (1 - z) * X_CHIPS + x
    across_right = (1 - z) * X_CHIPS + (x + 1) % X_CHIPS
    across_left = (1 - z) * X_CHIPS + (x + 3) % X_CHIPS
    across_far = (1 - z) * X_CHIPS + (x + 2) % X_CHIPS

    barrier = pltpu.get_barrier_semaphore()
    for peer in (left, right, across):
        pl.semaphore_signal(barrier, inc=1, device_id={"tp": peer}, device_id_type=MESH)
    loads = [
        pltpu.make_async_copy(cot_in, cot, load_sems.at[0]),
        pltpu.make_async_copy(wo_in, w_o, load_sems.at[1]),
        pltpu.make_async_copy(x_in, x_all.at[me], load_sems.at[2]),
        pltpu.make_async_copy(wq_in, w_qkv.at[:, pl.ds(0, Q_COLS)], load_sems.at[3]),
        pltpu.make_async_copy(wk_in, w_qkv.at[:, pl.ds(Q_COLS, HEAD)], load_sems.at[4]),
        pltpu.make_async_copy(wv_in, w_qkv.at[:, pl.ds(Q_COLS + HEAD, HEAD)], load_sems.at[5]),
    ]
    pl.semaphore_wait(barrier, 3)

    def remote(src, dst, peer, index):
        return pltpu.make_async_remote_copy(
            src_ref=src, dst_ref=dst, send_sem=send_sems.at[index], recv_sem=recv_sems.at[index],
            device_id={"tp": peer}, device_id_type=MESH,
        )

    upper, lower = pl.ds(0, TOKENS // 2), pl.ds(TOKENS // 2, TOKENS // 2)
    own = x_all.at[me]
    to_right = remote(x_in, own, right, 0)
    to_left = remote(x_in, own, left, 1)
    to_across = remote(x_in, own, across, 2)
    part = x_all.at[left, upper]
    far_right = remote(part, part, right, 3)
    part = x_all.at[right, lower]
    far_left = remote(part, part, left, 4)
    part = x_all.at[across]
    across_to_right = remote(part, part, right, 5)
    across_to_left = remote(part, part, left, 6)
    part = x_all.at[far]
    far_to_across = remote(part, part, across, 7)

    to_right.start()
    to_left.start()
    to_across.start()
    for load in loads:
        load.start()
    for load in loads[:2]:
        load.wait()

    acc[:, :Q_COLS] = jnp.zeros((TOKENS, Q_COLS), F32)

    @pl.loop(0, TP)
    def _(step):
        columns = pl.ds(pl.multiple_of(step * SLAB, SLAB), SLAB)
        acc[:, :Q_COLS] += dot(cot[:, columns], w_o[:, columns], (1, 1))

    d_mixed[...] = (acc[:, :Q_COLS] * SCALE).astype(BF16)

    for load in loads[2:]:
        load.wait()
    stores = []

    def project(block, index):
        store = pltpu.make_async_copy(x_all.at[block], x_out.at[block], store_sems.at[index])
        store.start()
        stores.append(store)
        rows = pl.ds(pl.multiple_of(block * SLAB, SLAB), SLAB)

        @pl.loop(0, QKV // 256)
        def _(step):
            columns = pl.ds(pl.multiple_of(step * 256, 256), 256)
            term = dot(x_all[block], w_qkv[rows, columns], (1, 0))
            if index == 0:
                acc[:, columns] = term
            else:
                acc[:, columns] += term

    project(me, 0)
    to_right.wait_recv()
    far_right.start()
    to_left.wait_recv()
    far_left.start()
    project(left, 1)
    to_across.wait_recv()
    across_to_right.start()
    across_to_left.start()
    project(right, 2)
    far_right.wait_recv()
    far_left.wait_recv()
    far_to_across.start()
    project(across, 3)
    project(far, 4)
    across_to_right.wait_recv()
    project(across_left, 5)
    across_to_left.wait_recv()
    project(across_right, 6)
    far_to_across.wait_recv()
    project(across_far, 7)

    cosine, sine = cos_ref[...], sin_ref[...]
    later = lax.broadcasted_iota(jnp.int32, (SEQ, SEQ), 0)
    earlier = lax.broadcasted_iota(jnp.int32, (SEQ, SEQ), 1)
    causal = earlier <= later
    heads = range(Q_HEADS)

    for sequence in range(SEQS):
        rows = slice(sequence * SEQ, (sequence + 1) * SEQ)

        def stacked(pieces):
            return jnp.concatenate(pieces, axis=0)

        queries = stacked(
            [
                turned(acc[rows, h * HEAD : (h + 1) * HEAD] * SCALE, cosine, sine).astype(BF16)
                for h in heads
            ]
        )
        keys = turned(acc[rows, Q_COLS : Q_COLS + HEAD] * SCALE, cosine, sine).astype(BF16)
        values = (acc[rows, Q_COLS + HEAD :] * SCALE).astype(BF16)
        number = jnp.broadcast_to(docs[sequence : sequence + 1, :].astype(F32), (SEQ, SEQ))
        allowed = jnp.logical_and(causal, number == number.T)
        scores = dot(queries, keys, (1, 1)) * SCORE_SCALE
        scores = stacked(
            [jnp.where(allowed, scores[h * SEQ : (h + 1) * SEQ], -1e9) for h in heads]
        )
        exps = jnp.exp(scores - jnp.max(scores, axis=1, keepdims=True))
        probs = exps / jnp.sum(exps, axis=1, keepdims=True)
        rounded = probs.astype(BF16)
        mixed = dot(rounded, values, (1, 0)).astype(BF16)
        d_heads = stacked([d_mixed[rows, h * HEAD : (h + 1) * HEAD] for h in heads])
        d_probs = dot(d_heads, values, (1, 1)).astype(BF16).astype(F32)
        d_values = dot(rounded, d_heads, (0, 0)).astype(BF16)
        d_scores = probs * (d_probs - jnp.sum(d_probs * probs, axis=1, keepdims=True))
        d_scores = (d_scores * SCORE_SCALE).astype(BF16)
        d_queries = dot(d_scores, keys, (1, 0)).astype(BF16).astype(F32)
        d_keys = dot(d_scores, queries, (0, 0)).astype(BF16).astype(F32)
        for h in heads:
            columns = slice(h * HEAD, (h + 1) * HEAD)
            stack = slice(h * SEQ, (h + 1) * SEQ)
            mixed_out[rows, columns] = mixed[stack]
            dqkv_out[rows, columns] = (turned(d_queries[stack], cosine, -sine) * SCALE).astype(BF16)
        dqkv_out[rows, Q_COLS : Q_COLS + HEAD] = (turned(d_keys, cosine, -sine) * SCALE).astype(BF16)
        dqkv_out[rows, Q_COLS + HEAD :] = (d_values.astype(F32) * SCALE).astype(BF16)

    for copy in (
        to_right, to_left, to_across, far_right, far_left,
        across_to_right, across_to_left, far_to_across,
    ):
        copy.wait_send()
    for store in stores:
        store.wait()


def front(normed, cotangent, w_query, w_key, w_value, w_out, documents):
    cosine, sine = rotation_tables()
    hbm = pl.BlockSpec(memory_space=pl.ANY)
    vmem = pl.BlockSpec(memory_space=pltpu.VMEM)
    return pl.pallas_call(
        front_kernel,
        name="gather_and_attend",
        out_shape=(
            jax.ShapeDtypeStruct((TP, TOKENS, SLAB), BF16),
            jax.ShapeDtypeStruct((TOKENS, Q_COLS), BF16),
            jax.ShapeDtypeStruct((TOKENS, QKV), BF16),
        ),
        in_specs=[hbm] * 6 + [vmem] * 3,
        out_specs=(hbm, vmem, vmem),
        scratch_shapes=[
            pltpu.VMEM((TP, TOKENS, SLAB), BF16),
            pltpu.VMEM((TOKENS, D), BF16),
            pltpu.VMEM((D, QKV), BF16),
            pltpu.VMEM((Q_COLS, D), BF16),
            pltpu.VMEM((TOKENS, QKV), F32),
            pltpu.VMEM((TOKENS, Q_COLS), BF16),
            pltpu.SemaphoreType.DMA((8,)),
            pltpu.SemaphoreType.DMA((8,)),
            pltpu.SemaphoreType.DMA((6,)),
            pltpu.SemaphoreType.DMA((8,)),
        ],
        compiler_params=pltpu.CompilerParams(
            collective_id=0, has_side_effects=True, vmem_limit_bytes=48 * 1024 * 1024
        ),
        cost_estimate=pl.CostEstimate(
            flops=6_000_000_000, bytes_accessed=20_000_000, transcendentals=300_000
        ),
    )(normed, cotangent, w_query, w_key, w_value, w_out, documents, cosine, sine)


def moved(weight, gradient, rate):
    gradient = gradient.astype(BF16).astype(F32)
    return (weight.astype(F32) - rate * gradient).astype(BF16)


def out_update_kernel(rate, mixed, cot, w_o, updated):
    gradient = dot(mixed[...], cot[...], (0, 0)) * SCALE
    updated[...] = moved(w_o[...], gradient, rate[0])


def out_update(rate, mixed, cotangent, w_out):
    width = 1024
    wide = pl.BlockSpec((TOKENS, width), lambda i: (0, i))
    return pl.pallas_call(
        out_update_kernel,
        name="update_out",
        grid=(D // width,),
        out_shape=jax.ShapeDtypeStruct((Q_COLS, D), BF16),
        in_specs=[
            pl.BlockSpec(memory_space=pltpu.SMEM),
            pl.BlockSpec((TOKENS, Q_COLS), lambda i: (0, 0)),
            wide,
            wide,
        ],
        out_specs=wide,
        compiler_params=pltpu.CompilerParams(vmem_limit_bytes=32 * 1024 * 1024),
        cost_estimate=pl.CostEstimate(
            flops=2 * TOKENS * Q_COLS * D, bytes_accessed=13_000_000, transcendentals=0
        ),
    )(rate, mixed, cotangent, w_out)


def in_update_kernel(rate, x_all, dqkv, w_q, w_k, w_v, new_q, new_k, new_v):
    gradient = dot(x_all[0], dqkv[...], (0, 0))
    new_q[...] = moved(w_q[...], gradient[:, :Q_COLS], rate[0])
    new_k[...] = moved(w_k[...], gradient[:, Q_COLS : Q_COLS + HEAD], rate[0])
    new_v[...] = moved(w_v[...], gradient[:, Q_COLS + HEAD :], rate[0])


def in_update(rate, x_all, dqkv, w_query, w_key, w_value):
    wide = pl.BlockSpec((SLAB, Q_COLS), lambda i: (i, 0))
    slim = pl.BlockSpec((SLAB, HEAD), lambda i: (i, 0))
    return pl.pallas_call(
        in_update_kernel,
        name="update_qkv",
        grid=(TP,),
        out_shape=(
            jax.ShapeDtypeStruct((D, Q_COLS), BF16),
            jax.ShapeDtypeStruct((D, HEAD), BF16),
            jax.ShapeDtypeStruct((D, HEAD), BF16),
        ),
        in_specs=[
            pl.BlockSpec(memory_space=pltpu.SMEM),
            pl.BlockSpec((1, TOKENS, SLAB), lambda i: (i, 0, 0)),
            pl.BlockSpec((TOKENS, QKV), lambda i: (0, 0)),
            wide,
            slim,
            slim,
        ],
        out_specs=(wide, slim, slim),
        compiler_params=pltpu.CompilerParams(vmem_limit_bytes=32 * 1024 * 1024),
        cost_estimate=pl.CostEstimate(
            flops=2 * TOKENS * QKV * D, bytes_accessed=18_000_000, transcendentals=0
        ),
    )(rate, x_all, dqkv, w_query, w_key, w_value)


def passed_along(value, distance):
    count = lax.axis_size("rep")
    pairs = [(source, (source + distance) % count) for source in range(count)]
    return lax.ppermute(value, "rep", pairs)


def average(own, peer):
    return (0.5 * (own.astype(F32) + peer.astype(F32))).astype(BF16)


def finish(distance, rate, x_all, mixed, dqkv, cotangent, w_query, w_key, w_value, w_out):
    new_o = out_update(rate, mixed, cotangent, w_out)
    peer_o = passed_along(new_o, distance)
    updated = in_update(rate, x_all, dqkv, w_query, w_key, w_value)
    peers = [passed_along(u, distance) for u in updated]
    partial = (jnp.dot(mixed, w_out, preferred_element_type=F32) * SCALE).astype(BF16)
    layer_out = lax.psum_scatter(
        partial.reshape(SEQS, SEQ, D), "tp", scatter_dimension=2, tiled=True
    )
    new = [average(u, p)[None] for u, p in zip((*updated, new_o), (*peers, peer_o))]
    return (layer_out, *new)


def per_device(normed, documents, cotangent, w_query, w_key, w_value, w_out, step_index):
    levels = lax.axis_size("rep").bit_length() - 1
    level = step_index[0] % levels
    rate = 3.0 * 32.0 / (32.0 + step_index.astype(F32))
    flat = cotangent.reshape(TOKENS, D)
    weights = (w_query[0], w_key[0], w_value[0], w_out[0])
    x_all, mixed, dqkv = front(normed.reshape(TOKENS, SLAB), flat, *weights, documents)
    return lax.switch(
        level,
        [functools.partial(finish, 2**exponent) for exponent in range(levels)],
        rate, x_all, mixed, dqkv, flat, *weights,
    )


def solution(mesh):
    in_specs = (
        P("rep", None, "tp"),
        P("rep", None),
        P("rep", None, None),
        P("rep", None, "tp"),
        P("rep", None, "tp"),
        P("rep", None, "tp"),
        P("rep", "tp", None),
        P(),
    )
    out_specs = (
        P("rep", None, "tp"),
        P("rep", None, "tp"),
        P("rep", None, "tp"),
        P("rep", None, "tp"),
        P("rep", "tp", None),
    )
    return jax.shard_map(
        per_device, mesh=mesh, in_specs=in_specs, out_specs=out_specs, check_vma=False
    )
```

time: 726 us -> 384 us (0.53)
  waiting for transfers between devices: 479 us -> 279 us
  other arithmetic: 122 us -> 9.85 us
  Pallas kernels: 0 us -> 53.6 us
  local copies, waits for them, and re-layouts: 56.8 us -> 3.41 us
  matrix products: 44.3 us -> 6.57 us
  loops' own time: 0.24 us -> 11.9 us
    ppermute x2 -> x4, waiting for transfers between devices: 441 us -> 216 us  [passed_along(): return lax.ppermute(value, 'rep', pairs)]
    reshape x2 -> x0, other arithmetic: 72.6 us -> none  [pack_all(): jnp.concatenate([member.reshape(-1) for member in members]).reshape(-1, 128)]
    pallas_call x0 -> x3, Pallas kernels: none -> 53.6 us  [the longest x1 41.4 us: front(): pl.pallas_call(front_kernel, name='gather_and_attend', out_shape=(jax.Sha...]
    convert_element_type x3 -> x0, other arithmetic: 42.1 us -> none  [the longest x1 40 us: per_device(): (0.5 * (own_updated.astype(jnp.float32) + peer_updated.astype(jnp.float32...]
    dot_general x15 -> x1, matrix products: 44.3 us -> 6.57 us  [finish(): jnp.dot(mixed, w_out, preferred_element_type=F32) * SCALE]
    reduce_scatter x1, waiting for transfers between devices: 37 us -> 62.3 us  [finish(): lax.psum_scatter(partial.reshape(SEQS, SEQ, D), 'tp', scatter_dimension=2...]
    unnamed x26 -> x12, local copies, waits for them, and re-layouts: 21.5 us -> 3.4 us
    another operation x3 -> x0, local copies, waits for them, and re-layouts: 17.8 us -> none  [the longest x1 7.51 us: per_device(): new_query[None]]
  transfers between devices with their start and end apart: 4 -> 5, of which waited for: 3 -> 3; matrix products, arithmetic and copies ran while one was open for 22% -> 3% of each run, Pallas kernels for 0% -> 3%
where the time goes in v1:
time: 384 us; the launch traced here: 383 us
  waiting for transfers between devices  279 us (73%)
  Pallas kernels  53.6 us (14%)
  between operations  14.9 us (4%)
  loops' own time  11.9 us (3%)
  other arithmetic  9.85 us (3%)
  matrix products  6.57 us (2%)
  starting transfers between devices  4.16 us (1%)
    ppermute x4, waiting for transfers between devices, passed_along(): return lax.ppermute(value, 'rep', pairs)  216 us
    reduce_scatter x1, waiting for transfers between devices, finish(): lax.psum_scatter(partial.reshape(SEQS, SEQ, D), 'tp', scatter_dimension=2...  62.3 us
    pallas_call x1, Pallas kernels, front(): pl.pallas_call(front_kernel, name='gather_and_attend', out_shape=(jax.Sha...  41.4 us
    another operation x1, loops' own time, per_device(): lax.switch(level, [functools.partial(finish, 2 ** exponent) for exponent...  11.9 us
    broadcast_in_dim x4, other arithmetic, finish(): average(u, p)[None]  9.85 us
  transfers between devices with their start and end apart: 5, of which 3 were waited for; matrix products, arithmetic and copies ran while one was open for 3% of the time, Pallas kernels for 3%

profile of v1, /device:TPU:1, one launch (start us, length us, event | category | flops | bytes accessed | tf_op | source)
XLA Modules:
  0.0 382.9 jit_solution(9710583892880187780)
XLA Ops:
  7.8 1.0 copy-done
  8.9 0.7 copy-done.1
  9.6 0.8 copy-done.2
  10.4 0.8 copy-done.3
  11.2 41.4 %gather_and_attend.1 = (bf16[8,512,512]{2,1,0:T(8,128)(2,1)}, bf16[512,512]{1,0:T(8,128)(2,1)S(1)}, bf16[512,768]{1,0:T(8,128)(2,1)S(1)}) custom-call(bf16[512,512]{1,0:T(8,128)(2,1)S(1)} %bitcast.54, bf16[512,4096]{1,0:T(8,128)(2,1)} %bitcast.55, bf16[4096,512]{1,0:T(8,128)(2,1)} %bitcast.69, bf16[4096,128]{1,0:T(8,128)(2,1)} %bitcast.74, ...), custom_call_target="tpu_custom_call" | custom-call | flops 6000000000 | bytes 20000000 | tf_op jit(solution)/shard_map/gather_and_attend/pallas_call | solution.py:218
  52.6 323.2 %conditional.1 = (bf16[4,128,512]{2,1,0:T(8,128)(2,1)}, bf16[1,4096,512]{2,1,0:T(8,128)(2,1)}, bf16[1,4096,128]{2,1,0:T(8,128)(2,1)}, bf16[1,4096,128]{2,1,0:T(8,128)(2,1)}, bf16[1,512,4096]{2,1,0:T(8,128)(2,1)}) conditional(s32[]{:T(128)} %clamp.3, (bf16[512,512]{1,0:T(8,128)(2,1)S(1)}, bf16[512,4096]{1,0:T(8,128)(2,1)}, ...), branch_computations={%region_0.2_spmd, %region_2.4_spmd, %region_4.6_spmd, %region_6.8_... | conditional | flops 7546601472 | bytes 161023744 | solution.py:346
  59.3 0.0 reduce-scatter.7.cloned.1.call-start
  59.3 6.6 %multiply_convert_fusion.7 = bf16[512,4096]{1,0:T(8,128)(2,1)} fusion(bf16[512,512]{1,0:T(8,128)(2,1)S(1)} %get-tuple-element.84.mixed, bf16[512,4096]{1,0:T(8,128)(2,1)} %get-tuple-element.85.w_o), kind=kOutput, calls=%fused_computation.11 | convolution fusion | flops 2151677952 | bytes 8912896 | tf_op jit(solution)/shard_map/cond/branch_1_fun/dot_general | solution.py:331
  65.9 0.0 reduce-scatter.7.cloned.1.call-update
  66.0 0.0 copy-start.5
  66.0 6.9 %update_out.5 = bf16[512,4096]{1,0:T(8,128)(2,1)S(1)} custom-call(f32[1]{0:T(128)S(6)} %div.5.rate, bf16[512,512]{1,0:T(8,128)(2,1)S(1)} %get-tuple-element.84.mixed, bf16[512,4096]{1,0:T(8,128)(2,1)} %get-tuple-element.95.cot, bf16[512,4096]{1,0:T(8,128)(2,1)} %get-tuple-element.85.w_o), custom_call_target="tpu_custom_call" | custom-call | flops 2147483648 | bytes 13000000 | tf_op jit(solution)/shard_map/cond/branch_1_fun/update_out/pallas_call | solution.py:262
  72.9 1.4 collective-permute-start.7
  74.2 5.3 %update_qkv.5 = (bf16[4096,512]{1,0:T(8,128)(2,1)S(1)}, bf16[4096,128]{1,0:T(8,128)(2,1)S(1)}, bf16[4096,128]{1,0:T(8,128)(2,1)S(1)}) custom-call(f32[1]{0:T(128)S(6)} %div.5.rate, bf16[8,512,512]{2,1,0:T(8,128)(2,1)S(1)} %copy-done.11, bf16[512,768]{1,0:T(8,128)(2,1)S(1)} %get-tuple-element.88.dqkv, bf16[4096,512]{1,0:T(8,128)(2,1)S(1)} %copy-done.5, ...), custom_call_target="tpu_custom_call" | custom-call | flops 3221225472 | bytes 18000000 | tf_op jit(solution)/shard_map/cond/branch_1_fun/update_qkv/pallas_call | solution.py:291
  79.6 1.4 collective-permute-start.5
  81.0 1.0 collective-permute-start.4
  82.0 0.4 collective-permute-start.6
  82.4 105.2 %collective-permute-done.5 = bf16[4096,128]{1,0:T(8,128)(2,1)S(1)} collective-permute-done((bf16[4096,128]{1,0:T(8,128)(2,1)S(1)}, bf16[4096,128]{1,0:T(8,128)(2,1)S(1)}, u32[]{:S(2)}, u32[]{:S(2)}) %collective-permute-start.5) | collective-permute-done | bytes 1048608 | tf_op jit(solution)/shard_map/cond/branch_1_fun/ppermute | solution.py:319
  187.6 1.3 fusion.6
  188.9 111.0 %collective-permute-done.6 = bf16[4096,128]{1,0:T(8,128)(2,1)S(1)} collective-permute-done((bf16[4096,128]{1,0:T(8,128)(2,1)S(1)}, bf16[4096,128]{1,0:T(8,128)(2,1)S(1)}, u32[]{:S(2)}, u32[]{:S(2)}) %collective-permute-start.6) | collective-permute-done | bytes 1048608 | tf_op jit(solution)/shard_map/cond/branch_1_fun/ppermute | solution.py:319
  299.9 1.3 fusion.7
  301.2 0.0 collective-permute-done.7
  301.2 3.6 fusion.5
  304.9 3.6 fusion.4
  308.5 62.3 %reduce-scatter.7.cloned.1.call-done = bf16[4,128,512]{2,1,0:T(8,128)(2,1)} async-done(((bf16[4,128,4096]{2,1,0:T(8,128)(2,1)}), bf16[4,128,512]{2,1,0:T(8,128)(2,1)}) %reduce-scatter.7.cloned.1.call-update) | async-done | bytes 524304 | tf_op jit(solution)/shard_map/cond/branch_1_fun/reduce_scatter | solution.py:332
  (12 shorter events, 0.0 us)
Async XLA Ops:
  7.8 1.0 copy-start
  8.9 0.7 copy-start.1
  9.6 0.8 copy-start.2
  10.4 0.8 copy-start.3
  11.2 41.4 %copy-start.8 = (bf16[1,4096,128]{2,1,0:T(8,128)(2,1)S(1)}, bf16[1,4096,128]{2,1,0:T(8,128)(2,1)}, u32[]{:S(2)}) copy-start(bf16[1,4096,128]{2,1,0:T(8,128)(2,1)} %param.18) | copy-start | bytes 3145732
  11.2 41.4 %copy-start.9 = (bf16[1,4096,128]{2,1,0:T(8,128)(2,1)S(1)}, bf16[1,4096,128]{2,1,0:T(8,128)(2,1)}, u32[]{:S(2)}) copy-start(bf16[1,4096,128]{2,1,0:T(8,128)(2,1)} %param.19) | copy-start | bytes 3145732
  59.3 311.5 %reduce-scatter.7.cloned.1.call-start = ((), (), s32[]{:S(2)}) async-start(), calls=%async_computation.5 | async-start | bytes 4718592 | tf_op jit(solution)/shard_map/cond/branch_1_fun/reduce_scatter | solution.py:332
  66.0 8.3 %copy-start.5 = (bf16[4096,512]{1,0:T(8,128)(2,1)S(1)}, bf16[4096,512]{1,0:T(8,128)(2,1)}, u32[]{:S(2)}) copy-start(bf16[4096,512]{1,0:T(8,128)(2,1)} %get-tuple-element.89.w_q) | copy-start | bytes 12582916 | tf_op jit(solution)/shard_map/cond
  66.0 8.3 %copy-start.11 = (bf16[8,512,512]{2,1,0:T(8,128)(2,1)S(1)}, bf16[8,512,512]{2,1,0:T(8,128)(2,1)}, u32[]{:S(2)}) copy-start(bf16[8,512,512]{2,1,0:T(8,128)(2,1)} %get-tuple-element.87.x_all) | copy-start | bytes 12582916 | tf_op jit(solution)/shard_map/cond
  72.9 228.3 %collective-permute-start.7 = (bf16[512,4096]{1,0:T(8,128)(2,1)S(1)}, bf16[512,4096]{1,0:T(8,128)(2,1)S(1)}, u32[]{:S(2)}, u32[]{:S(2)}) collective-permute-start(bf16[512,4096]{1,0:T(8,128)(2,1)S(1)} %update_out.5), channel_id=1, source_target_pairs={{0,16},{8,24},{16,32},{24,40},{32,48},{40,56},{48,64},{56,72},{64,... | collective-permute-start | bytes 12582920 | tf_op jit(solution)/shard_map/cond/branch_1_fun/ppermute | solution.py:319
  79.6 108.0 %collective-permute-start.5 = (bf16[4096,128]{1,0:T(8,128)(2,1)S(1)}, bf16[4096,128]{1,0:T(8,128)(2,1)S(1)}, u32[]{:S(2)}, u32[]{:S(2)}) collective-permute-start(bf16[4096,128]{1,0:T(8,128)(2,1)S(1)} %get-tuple-element.93), channel_id=1, source_target_pairs={{0,16},{8,24},{16,32},{24,40},{32,48},{40,56},{48,64},{56,72},{64,... | collective-permute-start | bytes 3145736 | tf_op jit(solution)/shard_map/cond/branch_1_fun/ppermute | solution.py:319
  81.0 223.9 %collective-permute-start.4 = (bf16[4096,512]{1,0:T(8,128)(2,1)S(1)}, bf16[4096,512]{1,0:T(8,128)(2,1)S(1)}, u32[]{:S(2)}, u32[]{:S(2)}) collective-permute-start(bf16[4096,512]{1,0:T(8,128)(2,1)S(1)} %get-tuple-element.92), channel_id=1, source_target_pairs={{0,16},{8,24},{16,32},{24,40},{32,48},{40,56},{48,64},{56,72},{64,... | collective-permute-start | bytes 12582920 | tf_op jit(solution)/shard_map/cond/branch_1_fun/ppermute | solution.py:319
  82.0 217.9 %collective-permute-start.6 = (bf16[4096,128]{1,0:T(8,128)(2,1)S(1)}, bf16[4096,128]{1,0:T(8,128)(2,1)S(1)}, u32[]{:S(2)}, u32[]{:S(2)}) collective-permute-start(bf16[4096,128]{1,0:T(8,128)(2,1)S(1)} %get-tuple-element.94), channel_id=1, source_target_pairs={{0,16},{8,24},{16,32},{24,40},{32,48},{40,56},{48,64},{56,72},{64,... | collective-permute-start | bytes 3145736 | tf_op jit(solution)/shard_map/cond/branch_1_fun/ppermute | solution.py:319
Sparse Core Ops, SparseCore 0:
  66.0 304.6 reduce-scatter.6

commit v2 on v1

v2 whole, which is shorter than its diff:
```python
import functools
import math

import jax
import jax.numpy as jnp
import numpy as np
from jax import lax
from jax.experimental import pallas as pl
from jax.experimental.pallas import tpu as pltpu
from jax.sharding import PartitionSpec as P

HEAD = 128
SEQS = 4
SEQ = 128
TOKENS = SEQS * SEQ
X_CHIPS = 4
Y_CHIPS = 4
TP = 8
D = 4096
SLAB = D // TP
Q_HEADS = 4
Q_COLS = Q_HEADS * HEAD
QKV = Q_COLS + 2 * HEAD
DIRECT_ROWS = 192
AROUND_ROWS = Q_COLS - DIRECT_ROWS
O_STEPS = 4
O_COLS = D // O_STEPS
WINDOW = 6
SCALE = 1.0 / math.sqrt(D)
SCORE_SCALE = 1.0 / math.sqrt(HEAD)
MESH = pl.DeviceIdType.MESH
F32 = jnp.float32
BF16 = jnp.bfloat16


def rotation_tables():
    half = HEAD // 2
    frequency = (500000.0 ** (-np.arange(half, dtype=np.float64) / half)).astype(np.float32)
    angles = np.arange(SEQ, dtype=np.float32)[:, None] * frequency[None, :]
    cosine, sine = np.cos(angles), np.sin(angles)
    return (
        np.concatenate([cosine, cosine], axis=1).astype(np.float32),
        np.concatenate([-sine, sine], axis=1).astype(np.float32),
    )


def dot(a, b, contract):
    return lax.dot_general(
        a, b, (((contract[0],), (contract[1],)), ((), ())), preferred_element_type=F32
    )


def turned(values, cosine, sine):
    return values * cosine + pltpu.roll(values, HEAD // 2, 1) * sine


def moved(weight, gradient, rate):
    gradient = gradient.astype(BF16).astype(F32)
    return (weight.astype(F32) - rate * gradient).astype(BF16)


def replica(z, y, core):
    return (z * Y_CHIPS + y) * 2 + core


def step_kernel(
    distance,
    x_in, cot_in, wq_in, wk_in, wv_in, wo_in, docs_in, cos_in, sin_in, rate_ref,
    layer_out, q_out, k_out, v_out, o_out,
    x_all, x_turned, cot, w_qkv, w_o, u_o, acc, d_mixed, dqkv, mixed_all, mixed_turned,
    docs, cos_ref, sin_ref, peer_o, peer_qkv, relay, partials, landed, across_sent, across_landed,
    send_sems, recv_sems, load_sems, o_sems, qkv_sems, relay_send, relay_recv,
    direct_send, direct_recv, sum_send, sum_recv, across_sems,
):
    me = lax.axis_index("tp")
    x, z = me % X_CHIPS, me // X_CHIPS
    right = z * X_CHIPS + (x + 1) % X_CHIPS
    left = z * X_CHIPS + (x + 3) % X_CHIPS
    far = z * X_CHIPS + (x + 2) % X_CHIPS
    across = (1 - z) * X_CHIPS + x
    across_right = (1 - z) * X_CHIPS + (x + 1) % X_CHIPS
    across_left = (1 - z) * X_CHIPS + (x + 3) % X_CHIPS
    across_far = (1 - z) * X_CHIPS + (x + 2) % X_CHIPS

    mine = lax.axis_index("rep")
    replicas = 2 * 2 * Y_CHIPS
    core, y, z_lo = mine % 2, mine // 2 % Y_CHIPS, mine // (2 * Y_CHIPS)
    target, origin = (mine + distance) % replicas, (mine + replicas - distance) % replicas
    around = distance <= 2
    back, ahead = (y + 3) % Y_CHIPS, (y + 1) % Y_CHIPS
    at_two, at_one = y // 2 * (1 - y % 2), (1 - y // 2) * (y % 2)
    hops_to = [
        replica(z_lo, back, core),
        replica((z_lo + at_two) % 2, back, core),
        replica(z_lo, back, core),
    ]
    hops_from = [
        replica(z_lo, ahead, core),
        replica((z_lo + at_one) % 2, ahead, core),
        replica(z_lo, ahead, core),
    ]
    if distance == 1:
        hops_to[2] = replica(z_lo, (y + 3 * core) % Y_CHIPS, 1 - core)
        hops_from[2] = replica(z_lo, (y + 1 - core) % Y_CHIPS, 1 - core)

    barrier = pltpu.get_barrier_semaphore()
    for peer in (left, right, far, across):
        pl.semaphore_signal(barrier, inc=1, device_id={"tp": peer}, device_id_type=MESH)
    senders = [origin] + (hops_from if around else [])
    for peer in senders:
        pl.semaphore_signal(barrier, inc=1, device_id={"rep": peer}, device_id_type=MESH)
    loads = [
        pltpu.make_async_copy(src, dst, load_sems.at[index])
        for index, (src, dst) in enumerate(
            (
                (cot_in, cot),
                (wo_in, w_o),
                (x_in, x_all.at[me]),
                (wq_in, w_qkv.at[:, pl.ds(0, Q_COLS)]),
                (wk_in, w_qkv.at[:, pl.ds(Q_COLS, HEAD)]),
                (wv_in, w_qkv.at[:, pl.ds(Q_COLS + HEAD, HEAD)]),
                (docs_in, docs),
                (cos_in, cos_ref),
                (sin_in, sin_ref),
            )
        )
    ]
    for load in loads[:2]:
        load.start()
    pl.semaphore_wait(barrier, 4 + len(senders))

    def remote(src, dst, peer, index):
        return pltpu.make_async_remote_copy(
            src_ref=src, dst_ref=dst, send_sem=send_sems.at[index], recv_sem=recv_sems.at[index],
            device_id={"tp": peer}, device_id_type=MESH,
        )

    upper, lower = pl.ds(0, TOKENS // 2), pl.ds(TOKENS // 2, TOKENS // 2)
    own = x_all.at[me]
    to_right = remote(x_in, own, right, 0)
    to_left = remote(x_in, own, left, 1)
    to_across = remote(x_in, own, across, 2)
    part = x_all.at[left, upper]
    far_right = remote(part, part, right, 3)
    part = x_all.at[right, lower]
    far_left = remote(part, part, left, 4)
    part = x_all.at[across]
    across_to_right = remote(part, part, right, 5)
    across_to_left = remote(part, part, left, 6)
    part = x_all.at[far]
    far_to_across = remote(part, part, across, 7)

    to_right.start()
    to_left.start()
    to_across.start()
    for load in loads[2:]:
        load.start()
    for load in loads[:2]:
        load.wait()

    acc[:, :Q_COLS] = jnp.zeros((TOKENS, Q_COLS), F32)

    @pl.loop(0, TP)
    def _(step):
        columns = pl.ds(pl.multiple_of(step * SLAB, SLAB), SLAB)
        acc[:, :Q_COLS] += dot(cot[:, columns], w_o[:, columns], (1, 1))

    d_mixed[...] = (acc[:, :Q_COLS] * SCALE).astype(BF16)

    for load in loads[2:]:
        load.wait()

    acc[...] = jnp.zeros((TOKENS, QKV), F32)
    order = (me, left, right, across, far, across_left, across_right, across_far)

    def on_step_1():
        to_right.wait_recv()
        far_right.start()
        to_left.wait_recv()
        far_left.start()

    def on_step_2():
        to_across.wait_recv()
        across_to_right.start()
        across_to_left.start()

    def on_step_3():
        far_right.wait_recv()
        far_left.wait_recv()
        far_to_across.start()

    arrivals = {
        1: on_step_1,
        2: on_step_2,
        3: on_step_3,
        5: across_to_right.wait_recv,
        6: across_to_left.wait_recv,
        7: far_to_across.wait_recv,
    }

    @pl.loop(0, TP)
    def _(turn):
        block = order[0]
        for index in range(1, TP):
            block = jnp.where(turn == index, order[index], block)
        for index, arrival in arrivals.items():
            pl.when(turn == index)(arrival)
        rows = pl.ds(pl.multiple_of(block * SLAB, SLAB), SLAB)

        @pl.loop(0, QKV // 256)
        def _(step):
            columns = pl.ds(pl.multiple_of(step * 256, 256), 256)
            acc[:, columns] += dot(x_all[block], w_qkv[rows, columns], (1, 0))

        x_turned[rows, :] = x_all[block].T

    cosine, sine = cos_ref[...], sin_ref[...]
    later = lax.broadcasted_iota(jnp.int32, (SEQ, SEQ), 0)
    earlier = lax.broadcasted_iota(jnp.int32, (SEQ, SEQ), 1)
    causal = earlier <= later
    heads = range(Q_HEADS)

    @pl.loop(0, SEQS)
    def _(sequence):
        rows = pl.ds(pl.multiple_of(sequence * SEQ, SEQ), SEQ)

        def stacked(pieces):
            return jnp.concatenate(pieces, axis=0)

        queries = stacked(
            [
                turned(acc[rows, h * HEAD : (h + 1) * HEAD] * SCALE, cosine, sine).astype(BF16)
                for h in heads
            ]
        )
        keys = turned(acc[rows, Q_COLS : Q_COLS + HEAD] * SCALE, cosine, sine).astype(BF16)
        values = (acc[rows, Q_COLS + HEAD :] * SCALE).astype(BF16)
        number = jnp.broadcast_to(docs[pl.ds(sequence, 1), :].astype(F32), (SEQ, SEQ))
        allowed = jnp.logical_and(causal, number == number.T)
        scores = dot(queries, keys, (1, 1)) * SCORE_SCALE
        scores = stacked(
            [jnp.where(allowed, scores[h * SEQ : (h + 1) * SEQ], -1e9) for h in heads]
        )
        exps = jnp.exp(scores - jnp.max(scores, axis=1, keepdims=True))
        probs = exps / jnp.sum(exps, axis=1, keepdims=True)
        rounded = probs.astype(BF16)
        mixed = dot(rounded, values, (1, 0)).astype(BF16)
        d_heads = stacked([d_mixed[rows, h * HEAD : (h + 1) * HEAD] for h in heads])
        d_probs = dot(d_heads, values, (1, 1)).astype(BF16).astype(F32)
        d_values = dot(rounded, d_heads, (0, 0)).astype(BF16)
        d_scores = probs * (d_probs - jnp.sum(d_probs * probs, axis=1, keepdims=True))
        d_scores = (d_scores * SCORE_SCALE).astype(BF16)
        d_queries = dot(d_scores, keys, (1, 0)).astype(BF16).astype(F32)
        d_keys = dot(d_scores, queries, (0, 0)).astype(BF16).astype(F32)
        for h in heads:
            columns = slice(h * HEAD, (h + 1) * HEAD)
            stack = slice(h * SEQ, (h + 1) * SEQ)
            mixed_all[rows, columns] = mixed[stack]
            mixed_turned[columns, rows] = mixed[stack].T
            dqkv[rows, columns] = (turned(d_queries[stack], cosine, -sine) * SCALE).astype(BF16)
        dqkv[rows, Q_COLS : Q_COLS + HEAD] = (turned(d_keys, cosine, -sine) * SCALE).astype(BF16)
        dqkv[rows, Q_COLS + HEAD :] = (d_values.astype(F32) * SCALE).astype(BF16)

    rate = rate_ref[0]
    top, bottom = pl.ds(0, DIRECT_ROWS), pl.ds(DIRECT_ROWS, AROUND_ROWS)
    direct_rows = top if around else pl.ds(0, Q_COLS)

    def o_columns(step):
        return pl.ds(pl.multiple_of(step * O_COLS, O_COLS), O_COLS)

    def qkv_rows(step):
        return pl.ds(pl.multiple_of(step * SLAB, SLAB), SLAB)

    def sent_to(src, dst, sems, index, peer):
        return pltpu.make_async_remote_copy(
            src_ref=src, dst_ref=dst, send_sem=sems[0].at[index], recv_sem=sems[1].at[index],
            device_id={"rep": peer}, device_id_type=MESH,
        )

    def direct_o(step):
        part = (direct_rows, o_columns(step))
        return sent_to(u_o.at[part], peer_o.at[part], (direct_send, direct_recv), step, target)

    def direct_qkv(step):
        rows = qkv_rows(step)
        return sent_to(
            w_qkv.at[rows, :], peer_qkv.at[rows, :],
            (direct_send, direct_recv), O_STEPS + step, target,
        )

    def relayed(hop, step, own=False):
        columns = o_columns(step)
        src = u_o.at[bottom, columns] if own or hop == 0 else relay.at[hop - 1, :, columns]
        dst = peer_o.at[bottom, columns] if hop == 2 else relay.at[hop, :, columns]
        return sent_to(src, dst, (relay_send, relay_recv), hop * O_STEPS + step, hops_to[hop])

    def relaying(action):
        if distance == 1:
            pl.when(core == 1)(action)
        else:
            action()

    @pl.loop(0, O_STEPS)
    def _(step):
        columns = o_columns(step)

        @pl.loop(0, O_COLS // SLAB)
        def _(half):
            piece = pl.ds(pl.multiple_of(step * O_COLS + half * SLAB, SLAB), SLAB)
            gradient = dot(mixed_turned[...], cot[:, piece], (1, 0)) * SCALE
            u_o[:, piece] = moved(w_o[:, piece], gradient, rate)
        if around:
            relaying(lambda: relayed(0, step).start())
        if distance == 1:
            pl.when(core == 0)(lambda: relayed(2, step, own=True).start())
        direct_o(step).start()

    @pl.loop(0, TP)
    def _(step):
        rows = qkv_rows(step)
        gradient = dot(x_turned[rows, :], dqkv[...], (1, 0))
        w_qkv[rows, :] = moved(w_qkv[rows, :], gradient, rate)

        @pl.when(step < WINDOW - O_STEPS)
        def _():
            direct_qkv(step).start()

    def partial(to_x, to_z, half):
        owner = to_z * X_CHIPS + to_x
        columns = pl.ds(pl.multiple_of(owner * SLAB + half * 256, 256), 256)
        return dot(mixed_all[...], w_o[:, columns], (1, 0)) * SCALE

    def half_slab(half):
        return pl.ds(pl.multiple_of(half * 256, 256), 256)

    def sum_copy(slot):
        to_x = (x + slot % 3 + 1) % X_CHIPS
        return pltpu.make_async_remote_copy(
            src_ref=partials.at[slot], dst_ref=landed.at[slot],
            send_sem=sum_send.at[slot], recv_sem=sum_recv.at[slot],
            device_id={"tp": z * X_CHIPS + to_x}, device_id_type=MESH,
        )

    @pl.loop(0, 6)
    def _(slot):
        to_x = (x + slot % 3 + 1) % X_CHIPS
        to_z = (z + 1 + slot // 3) % 2

        @pl.loop(0, 2)
        def _(half):
            partials[slot, :, half_slab(half)] = partial(to_x, to_z, half).astype(BF16)

        sum_copy(slot).start()

    def summed(plane, to_z, into, extra=None):
        for slot in range(plane * 3, plane * 3 + 3):
            sum_copy(slot).wait_recv()

        @pl.loop(0, 2)
        def _(half):
            columns = half_slab(half)
            total = partial(x, to_z, half)
            for slot in range(plane * 3, plane * 3 + 3):
                total += landed[slot, :, columns].astype(F32)
            if extra is not None:
                total += extra[:, columns].astype(F32)
            into[:, columns] = total.astype(BF16)

    crossing = pltpu.make_async_remote_copy(
        src_ref=across_sent, dst_ref=across_landed,
        send_sem=across_sems.at[0], recv_sem=across_sems.at[1],
        device_id={"tp": across}, device_id_type=MESH,
    )

    def cross():
        summed(0, 1 - z, across_sent)
        crossing.start()

    def finish_output():
        crossing.wait_recv()
        summed(1, z, layer_out, across_landed)

    def averaged(own, peer, first_row, rows, columns):
        @pl.loop(0, rows // 16)
        def _(step):
            part = pl.ds(pl.multiple_of(first_row + step * 16, 16), 16)
            total = own[part, columns].astype(F32) + peer[part, columns].astype(F32)
            peer[part, columns] = (0.5 * total).astype(BF16)

    def store_o(step, index, rows):
        part = (rows, o_columns(step))
        return pltpu.make_async_copy(peer_o.at[part], o_out.at[part], o_sems.at[step, index])

    def stores_qkv(step):
        rows = qkv_rows(step)
        return [
            pltpu.make_async_copy(
                peer_qkv.at[rows, pl.ds(start, out.shape[1])], out.at[rows, :],
                qkv_sems.at[step, index],
            )
            for index, (start, out) in enumerate(
                ((0, q_out), (Q_COLS, k_out), (Q_COLS + HEAD, v_out))
            )
        ]

    def arrived(index):
        if index + WINDOW < O_STEPS + TP:
            direct_qkv(index + WINDOW - O_STEPS).start()
        if index < O_STEPS:
            direct_o(index).wait_recv()
            averaged(u_o, peer_o, 0, DIRECT_ROWS if around else Q_COLS, o_columns(index))
            store_o(index, 0, direct_rows).start()
        else:
            step = index - O_STEPS
            direct_qkv(step).wait_recv()
            averaged(w_qkv, peer_qkv, step * SLAB, SLAB, slice(None))
            for store in stores_qkv(step):
                store.start()

    def pass_on(hop):
        def action():
            @pl.loop(0, O_STEPS)
            def _(step):
                relayed(hop - 1, step).wait_recv()
                relayed(hop, step).start()

        relaying(action)

    events = {
        1: {4: [lambda: pass_on(1)], 7: [cross, lambda: pass_on(2)]},
        2: {4: [lambda: pass_on(1), cross], 7: [lambda: pass_on(2)]},
        4: {1: [cross]},
        8: {1: [cross]},
    }[distance]
    for index in range(O_STEPS + TP):
        arrived(index)
        for event in events.get(index, ()):
            event()

    finish_output()
    if around:
        for step in range(O_STEPS):
            relayed(2, step).wait_recv()
            averaged(u_o, peer_o, DIRECT_ROWS, AROUND_ROWS, o_columns(step))
            store_o(step, 1, bottom).start()

    for step in range(O_STEPS):
        direct_o(step).wait_send()
        store_o(step, 0, direct_rows).wait()
        if around:
            store_o(step, 1, bottom).wait()
            relayed(2, step).wait_send()
    for step in range(TP):
        direct_qkv(step).wait_send()
        for store in stores_qkv(step):
            store.wait()
    if around:

        def relays_sent():
            for step in range(O_STEPS):
                relayed(0, step).wait_send()
                relayed(1, step).wait_send()

        relaying(relays_sent)
    for copy in (
        to_right, to_left, to_across, far_right, far_left,
        across_to_right, across_to_left, far_to_across, *map(sum_copy, range(6)), crossing,
    ):
        copy.wait_send()


def step(distance, normed, cotangent, w_query, w_key, w_value, w_out, documents, rate):
    cosine, sine = rotation_tables()
    hbm = pl.BlockSpec(memory_space=pl.ANY)
    vmem = pl.BlockSpec(memory_space=pltpu.VMEM)
    dma = pltpu.SemaphoreType.DMA
    block = (TOKENS, SLAB)
    layer_out, *new = pl.pallas_call(
        functools.partial(step_kernel, distance),
        name="step_%d" % distance,
        out_shape=(
            jax.ShapeDtypeStruct(block, BF16),
            jax.ShapeDtypeStruct((D, Q_COLS), BF16),
            jax.ShapeDtypeStruct((D, HEAD), BF16),
            jax.ShapeDtypeStruct((D, HEAD), BF16),
            jax.ShapeDtypeStruct((Q_COLS, D), BF16),
        ),
        in_specs=[hbm] * 9 + [pl.BlockSpec(memory_space=pltpu.SMEM)],
        out_specs=(vmem, hbm, hbm, hbm, hbm),
        scratch_shapes=[
            pltpu.VMEM((TP, TOKENS, SLAB), BF16),
            pltpu.VMEM((D, TOKENS), BF16),
            pltpu.VMEM((TOKENS, D), BF16),
            pltpu.VMEM((D, QKV), BF16),
            pltpu.VMEM((Q_COLS, D), BF16),
            pltpu.VMEM((Q_COLS, D), BF16),
            pltpu.VMEM((TOKENS, QKV), F32),
            pltpu.VMEM((TOKENS, Q_COLS), BF16),
            pltpu.VMEM((TOKENS, QKV), BF16),
            pltpu.VMEM((TOKENS, Q_COLS), BF16),
            pltpu.VMEM((Q_COLS, TOKENS), BF16),
            pltpu.VMEM((SEQS, SEQ), jnp.int32),
            pltpu.VMEM((SEQ, HEAD), F32),
            pltpu.VMEM((SEQ, HEAD), F32),
            pltpu.VMEM((Q_COLS, D), BF16),
            pltpu.VMEM((D, QKV), BF16),
            pltpu.VMEM((2, AROUND_ROWS, D), BF16) if distance <= 2 else pltpu.VMEM((2, 16, 128), BF16),
            pltpu.VMEM((6, *block), BF16),
            pltpu.VMEM((6, *block), BF16),
            pltpu.VMEM(block, BF16),
            pltpu.VMEM(block, BF16),
            dma((8,)),
            dma((8,)),
            dma((9,)),
            dma((O_STEPS, 2)),
            dma((TP, 3)),
            dma((3 * O_STEPS,)),
            dma((3 * O_STEPS,)),
            dma((O_STEPS + TP,)),
            dma((O_STEPS + TP,)),
            dma((6,)),
            dma((6,)),
            dma((2,)),
        ],
        compiler_params=pltpu.CompilerParams(
            collective_id=distance, has_side_effects=True, vmem_limit_bytes=62 * 1024 * 1024
        ),
        cost_estimate=pl.CostEstimate(
            flops=14_000_000_000, bytes_accessed=30_000_000, transcendentals=300_000
        ),
    )(normed, cotangent, w_query, w_key, w_value, w_out, documents, cosine, sine, rate)
    return (layer_out.reshape(SEQS, SEQ, SLAB), *(n[None] for n in new))


def per_device(normed, documents, cotangent, w_query, w_key, w_value, w_out, step_index):
    levels = lax.axis_size("rep").bit_length() - 1
    level = step_index[0] % levels
    rate = 3.0 * 32.0 / (32.0 + step_index.astype(F32))
    return lax.switch(
        level,
        [functools.partial(step, 2**exponent) for exponent in range(levels)],
        normed.reshape(TOKENS, SLAB), cotangent.reshape(TOKENS, D),
        w_query[0], w_key[0], w_value[0], w_out[0], documents, rate,
    )


def solution(mesh):
    in_specs = (
        P("rep", None, "tp"),
        P("rep", None),
        P("rep", None, None),
        P("rep", None, "tp"),
        P("rep", None, "tp"),
        P("rep", None, "tp"),
        P("rep", "tp", None),
        P(),
    )
    out_specs = (
        P("rep", None, "tp"),
        P("rep", None, "tp"),
        P("rep", None, "tp"),
        P("rep", None, "tp"),
        P("rep", "tp", None),
    )
    return jax.shard_map(
        per_device, mesh=mesh, in_specs=in_specs, out_specs=out_specs, check_vma=False
    )
```

time: 384 us -> 298 us (0.78)
  waiting for transfers between devices: 279 us -> 0 us
  Pallas kernels: 53.6 us -> 287 us
  between operations: 14.9 us -> 1.35 us
  loops' own time: 11.9 us -> 0.43 us
  other arithmetic: 9.85 us -> 0 us
  matrix products: 6.57 us -> 0 us
  local copies, waits for them, and re-layouts: 3.41 us -> 9.39 us
  starting transfers between devices: 4.16 us -> 0 us
    pallas_call x3 -> x1, Pallas kernels: 53.6 us -> 287 us  [step(): pl.pallas_call(functools.partial(step_kernel, distance), name='step_%d' %...]
    ppermute x4 -> x0, waiting for transfers between devices: 216 us -> none  [passed_along(): return lax.ppermute(value, 'rep', pairs)]
    reduce_scatter x1 -> x0, waiting for transfers between devices: 62.3 us -> none  [finish(): lax.psum_scatter(partial.reshape(SEQS, SEQ, D), 'tp', scatter_dimension=2...]
    another operation x1, loops' own time: 11.9 us -> 0.43 us  [per_device(): lax.switch(level, [functools.partial(step, 2 ** exponent) for exponent in...]
    broadcast_in_dim x4 -> x0, other arithmetic: 9.85 us -> none  [finish(): average(u, p)[None]]
    dot_general x1 -> x0, matrix products: 6.57 us -> none  [finish(): jnp.dot(mixed, w_out, preferred_element_type=F32) * SCALE]
    unnamed x12 -> x9, local copies, waits for them, and re-layouts: 3.4 us -> 9.39 us
    ppermute x4 -> x0, starting transfers between devices: 4.12 us -> none  [passed_along(): return lax.ppermute(value, 'rep', pairs)]
  transfers between devices with their start and end apart: 5 -> 0, of which waited for: 3 -> 0; matrix products, arithmetic and copies ran while one was open for 3% -> 0% of each run, Pallas kernels for 3% -> 0%
where the time goes in v2:
time: 298 us
  Pallas kernels  287 us (96%)
  local copies, waits for them, and re-layouts  9.39 us (3%)
    pallas_call x1, Pallas kernels, step(): pl.pallas_call(functools.partial(step_kernel, distance), name='step_%d' %...  287 us
    unnamed x9, local copies, waits for them, and re-layouts  9.39 us

profile of v2, /device:TPU:1, one launch (start us, length us, event | category | flops | bytes accessed | tf_op | source)
XLA Modules:
  0.0 298.0 jit_solution(6200651161051360929)
XLA Ops:
  1.3 287.2 %conditional.1 = ((bf16[512,512]{1,0:T(8,128)(2,1)S(1)}, bf16[4096,512]{1,0:T(8,128)(2,1)}, bf16[4096,128]{1,0:T(8,128)(2,1)S(1)}, bf16[4096,128]{1,0:T(8,128)(2,1)}, bf16[512,4096]{1,0:T(8,128)(2,1)})) conditional(s32[]{:T(128)} %clamp.3, (bf16[512,512]{1,0:T(8,128)(2,1)}, bf16[512,4096]{1,0:T(8,128)(2,1)}, ...), branch_computations={%region_0.1_spmd, %region_1.2_spmd, %region_2.3_spmd, %region_3.4_... | conditional | flops 14000000000 | bytes 30000008 | solution.py:539
  1.5 286.8 %step_4.1 = (bf16[512,512]{1,0:T(8,128)(2,1)S(1)}, bf16[4096,512]{1,0:T(8,128)(2,1)}, bf16[4096,128]{1,0:T(8,128)(2,1)S(1)}, bf16[4096,128]{1,0:T(8,128)(2,1)}, bf16[512,4096]{1,0:T(8,128)(2,1)}) custom-call(bf16[512,512]{1,0:T(8,128)(2,1)} %get-tuple-element.110.x_in, bf16[512,4096]{1,0:T(8,128)(2,1)} %get-tuple-element.111.cot_in, ...), custom_call_target="tpu_custom_call" | custom-call | flops 14000000000 | bytes 30000000 | tf_op jit(solution)/shard_map/cond/branch_2_fun/step_4/pallas_call | solution.py:478
  288.6 0.8 copy.47
  289.4 0.0 copy-start.1
  289.4 0.0 copy-start
  289.4 4.6 %copy.48 = bf16[1,4096,512]{2,1,0:T(8,128)(2,1)} copy(bf16[1,4096,512]{2,1,0:T(8,128)(2,1)} %bitcast.15) | data formatting | bytes 8388608
  294.0 1.0 copy.49
  295.0 0.0 copy-done.1
  295.0 1.0 copy.50
  295.9 0.0 copy-done
  295.9 2.0 copy.51
Async XLA Ops:
  289.4 5.6 %copy-start.1 = (bf16[4096,128]{1,0:T(8,128)(2,1)S(1)}, bf16[4096,128]{1,0:T(8,128)(2,1)}, u32[]{:S(2)}) copy-start(bf16[4096,128]{1,0:T(8,128)(2,1)} %get-tuple-element.147) | copy-start | bytes 3145732
  289.4 6.6 %copy-start = (bf16[512,4096]{1,0:T(8,128)(2,1)S(1)}, bf16[512,4096]{1,0:T(8,128)(2,1)}, u32[]{:S(2)}) copy-start(bf16[512,4096]{1,0:T(8,128)(2,1)} %get-tuple-element.146) | copy-start | bytes 12582916
